TPU v7x, 128 devices: a whole 4x4x4 slice. The times are simulated.
128 devices in a mesh: dp: 16 (over y, x_hi, core), mp: 8 (over z, x_lo).
Axes of the slice: x: 4 (x_hi: 2, x_lo: 2; x = x_hi * 2 + x_lo), y: 4, z: 4, core: 2. Of those that a mesh axis runs over, the one named last changes fastest.
Arguments:
- tokens: bfloat16 [2, 8192, 1024], P(None, ('dp', 'mp')), may hold values from -6 to 6
- segment_ids: int32 [2, 8192], P(None, 'dp'), may hold values from 0 to 3, as said below
- cotangent: bfloat16 [2, 8192, 1024], P(None, ('dp', 'mp')), may hold values from -6 to 6
- w_query: bfloat16 [1024, 1024], P('dp', 'mp'), may hold values from -0.1875 to 0.1875
- w_key: bfloat16 [1024, 512], P('dp', 'mp'), may hold values from -0.1875 to 0.1875
- w_value: bfloat16 [1024, 512], P('dp', 'mp'), may hold values from -0.1875 to 0.1875
- w_out: bfloat16 [1024, 1024], P('mp', 'dp'), may hold values from -1.5 to 1.5
- w_gate: bfloat16 [1024, 4608], P('dp', 'mp'), may hold values from -0.1875 to 0.1875
- w_up: bfloat16 [1024, 4608], P('dp', 'mp'), may hold values from -0.1875 to 0.1875
- w_down: bfloat16 [4608, 1024], P('mp', 'dp'), may hold values from -0.09375 to 0.09375
- norm_gain: float32 [1024], replicated, may hold values from 0.5 to 1.5
- ffn_gain: float32 [1024], replicated, may hold values from 0.5 to 1.5
- query_gain: float32 [64], replicated, may hold values from 0.1 to 1.9
- key_gain: float32 [64], replicated, may hold values from 0.1 to 1.9
Outputs:
- output: bfloat16 [2, 8192, 1024], P(None, ('dp', 'mp'))
- input_grad: bfloat16 [2, 8192, 1024], P(None, ('dp', 'mp'))
- grad_query: float32 [1024, 1024], P('dp', 'mp')
- grad_key: float32 [1024, 512], P('dp', 'mp')
- grad_value: float32 [1024, 512], P('dp', 'mp')
- grad_out: float32 [1024, 1024], P('mp', 'dp')
- grad_gate: float32 [1024, 4608], P('dp', 'mp')
- grad_up: float32 [1024, 4608], P('dp', 'mp')
- grad_down: float32 [4608, 1024], P('mp', 'dp')
- grad_norm: float32 [1024], replicated
- grad_ffn_norm: float32 [1024], replicated
- grad_query_gain: float32 [64], replicated
- grad_key_gain: float32 [64], replicated
Inputs may be any that keep to these rules, and one draw needn't show every extreme that they name: `segment_ids`: in each micro-batch each data group's 512 tokens hold 1 to 4 whole sequences, numbered 0, 1, ... in order; in each micro-batch some group holds a single sequence and some group holds four.
All inputs are finite; a program needn't handle non-finite values.
Results may differ from a plain program's by a relative error of at most 0.025.
Values may be sent and summed in bfloat16 or wider, within the bound.
No kernel may reach another device: no remote copies, remote signals or barrier semaphores. Data moves between devices by JAX's collectives and lax.ppermute only.
A program may use at most 128 MiB of HBM per device.

v0:
```python
import jax
import jax.numpy as jnp
from jax import lax
from jax.sharding import PartitionSpec as P

eps = 1e-05
rope_base = 1000000.0


def product(left, right):
    return jnp.dot(left, right, preferred_element_type=jnp.float32)


def product_nt(left, right):
    return lax.dot_general(
        left, right, (((1,), (1,)), ((), ())), preferred_element_type=jnp.float32
    )


def product_tn(left, right):
    return lax.dot_general(
        left, right, (((0,), (0,)), ((), ())), preferred_element_type=jnp.float32
    )


def rms_rows(value, gain):
    return value * lax.rsqrt(jnp.mean(value * value, axis=-1, keepdims=True) + eps) * gain


def rotate(value, cosine, sine):
    half = value.shape[-1] // 2
    turned = jnp.concatenate([-value[..., half:], value[..., :half]], axis=-1)
    return value * cosine + turned * sine


def head_prepare(raw, gain, cosine, sine):
    return rotate(rms_rows(raw, gain), cosine, sine)


def rope_tables(segment, head_size):
    count = segment.shape[0]
    index = jnp.arange(count, dtype=jnp.int32)
    change = jnp.concatenate([jnp.ones((1,), dtype=bool), segment[1:] != segment[:-1]])
    start = lax.cummax(jnp.where(change, index, 0), axis=0)
    place = (index - start).astype(jnp.float32)
    freq = rope_base ** (-(jnp.arange(head_size // 2, dtype=jnp.float32) * 2.0 / head_size))
    angle = place[:, None] * freq[None, :]
    angle = jnp.concatenate([angle, angle], axis=-1)
    return (jnp.cos(angle)[:, None, :], jnp.sin(angle)[:, None, :])


def collect(w_query, w_key, w_value, w_gate, w_up, w_out, w_down):
    rows_full = (
        lax.all_gather(w_query, "dp", axis=0, tiled=True),
        lax.all_gather(w_key, "dp", axis=0, tiled=True),
        lax.all_gather(w_value, "dp", axis=0, tiled=True),
        lax.all_gather(w_gate, "dp", axis=0, tiled=True),
        lax.all_gather(w_up, "dp", axis=0, tiled=True),
    )
    cols_full = (
        lax.all_gather(w_out, "dp", axis=1, tiled=True),
        lax.all_gather(w_down, "dp", axis=1, tiled=True),
    )
    return tuple(rows_full) + tuple(cols_full)


def reduce_grads(grads):
    rows_part = (
        lax.psum_scatter(
            grads[0].astype(jnp.bfloat16), "dp", scatter_dimension=0, tiled=True
        ).astype(jnp.float32),
        lax.psum_scatter(
            grads[1].astype(jnp.bfloat16), "dp", scatter_dimension=0, tiled=True
        ).astype(jnp.float32),
        lax.psum_scatter(
            grads[2].astype(jnp.bfloat16), "dp", scatter_dimension=0, tiled=True
        ).astype(jnp.float32),
        lax.psum_scatter(
            grads[3].astype(jnp.bfloat16), "dp", scatter_dimension=0, tiled=True
        ).astype(jnp.float32),
        lax.psum_scatter(
            grads[4].astype(jnp.bfloat16), "dp", scatter_dimension=0, tiled=True
        ).astype(jnp.float32),
    )
    cols_part = (
        lax.psum_scatter(
            grads[5].astype(jnp.bfloat16), "dp", scatter_dimension=1, tiled=True
        ).astype(jnp.float32),
        lax.psum_scatter(
            grads[6].astype(jnp.bfloat16), "dp", scatter_dimension=1, tiled=True
        ).astype(jnp.float32),
    )
    return tuple(rows_part) + tuple(cols_part)


def block_scores(queries, keys, allowed, scale):
    scores = jnp.einsum("bgrd,kgd->grbk", queries, keys, preferred_element_type=jnp.float32) * scale
    return jnp.where(allowed[None, None], scores, -1e30)


def attend(queries, keys, values, allowed, scale):
    scores = block_scores(queries, keys, allowed, scale)
    top = jnp.max(scores, axis=-1, keepdims=True)
    expo = jnp.exp(scores - top)
    total = jnp.sum(expo, axis=-1, keepdims=True)
    weights = (expo / total).astype(jnp.bfloat16)
    pieces = jnp.einsum("grbk,kgd->bgrd", weights, values, preferred_element_type=jnp.float32)
    kept = [(top, total)]
    return (pieces, kept)


def attend_back(queries, keys, values, allowed, scale, kept, grad_mixed):
    top, total = kept[0]
    scores = block_scores(queries, keys, allowed, scale)
    soft = jnp.exp(scores - top) / total
    soft_low = soft.astype(jnp.bfloat16)
    grad_weights = jnp.einsum(
        "bgrd,kgd->grbk", grad_mixed, values, preferred_element_type=jnp.float32
    )
    center = jnp.sum(soft * grad_weights, axis=-1, keepdims=True)
    grad_scores = (soft * (grad_weights - center)).astype(jnp.bfloat16)
    grad_query_parts = (
        jnp.einsum("grbk,kgd->bgrd", grad_scores, keys, preferred_element_type=jnp.float32) * scale
    )
    key_term = (
        jnp.einsum("grbk,bgrd->kgd", grad_scores, queries, preferred_element_type=jnp.float32)
        * scale
    )
    value_term = jnp.einsum(
        "grbk,bgrd->kgd", soft_low, grad_mixed, preferred_element_type=jnp.float32
    )
    return (grad_query_parts, key_term, value_term)


def local(
    tokens,
    segment_ids,
    cotangent,
    w_query,
    w_key,
    w_value,
    w_out,
    w_gate,
    w_up,
    w_down,
    norm_gain,
    ffn_gain,
    query_gain,
    key_gain,
):
    micro = tokens.shape[0]
    width = tokens.shape[2]
    head_size = query_gain.shape[0]
    local_heads = w_query.shape[1] // head_size
    local_kv = w_key.shape[1] // head_size
    repeat = local_heads // local_kv
    group = segment_ids.shape[1]
    scale = head_size ** (-0.5)
    shard_list = (w_query, w_key, w_value, w_gate, w_up, w_out, w_down)
    totals = tuple((jnp.zeros((width, w.shape[1]), jnp.float32) for w in shard_list[:5])) + tuple(
        (jnp.zeros((w.shape[0], width), jnp.float32) for w in shard_list[5:])
    )
    gain_totals = (
        jnp.zeros_like(norm_gain),
        jnp.zeros_like(ffn_gain),
        jnp.zeros_like(query_gain),
        jnp.zeros_like(key_gain),
    )
    outputs = []
    input_grads = []
    for micro_index in range(micro):
        full = collect(w_query, w_key, w_value, w_gate, w_up, w_out, w_down)
        query_full, key_full, value_full, gate_full, up_full, out_full, down_full = full
        segment = segment_ids[micro_index]
        cosine, sine = rope_tables(segment, head_size)
        index = jnp.arange(group, dtype=jnp.int32)
        allowed = (segment[:, None] == segment[None, :]) & (index[:, None] >= index[None, :])
        resid = tokens[micro_index].astype(jnp.float32)
        normed_local = rms_rows(resid, norm_gain)
        normed = lax.all_gather(normed_local.astype(jnp.bfloat16), "mp", axis=0, tiled=True)
        query_raw = product(normed, query_full).reshape(group, local_heads, head_size)
        key_raw = product(normed, key_full).reshape(group, local_kv, head_size)
        values = (
            product(normed, value_full).astype(jnp.bfloat16).reshape(group, local_kv, head_size)
        )
        queries = (
            head_prepare(query_raw, query_gain, cosine, sine)
            .astype(jnp.bfloat16)
            .reshape(group, local_kv, repeat, head_size)
        )
        keys = head_prepare(key_raw, key_gain, cosine, sine).astype(jnp.bfloat16)
        mixed_raw, kept = attend(queries, keys, values, allowed, scale)
        mixed = mixed_raw.reshape(group, local_heads * head_size).astype(jnp.bfloat16)
        hidden_state = resid + lax.psum_scatter(
            product(mixed, out_full).astype(jnp.bfloat16), "mp", scatter_dimension=0, tiled=True
        ).astype(jnp.float32)
        second_local = rms_rows(hidden_state, ffn_gain)
        second = lax.all_gather(second_local.astype(jnp.bfloat16), "mp", axis=0, tiled=True)
        gate = product(second, gate_full)
        up_act = product(second, up_full)
        inner = (jax.nn.silu(gate) * up_act).astype(jnp.bfloat16)
        result = hidden_state + lax.psum_scatter(
            product(inner, down_full).astype(jnp.bfloat16), "mp", scatter_dimension=0, tiled=True
        ).astype(jnp.float32)
        outputs.append(result.astype(jnp.bfloat16))
        upstream = lax.all_gather(cotangent[micro_index], "mp", axis=0, tiled=True)
        grad_down = product_tn(inner, upstream)
        grad_inner = product_nt(upstream, down_full)
        glu_value, glu_pull = jax.vjp(
            lambda gate_in, up_in: jax.nn.silu(gate_in) * up_in, gate, up_act
        )
        grad_gate_act, grad_up_act = glu_pull(grad_inner)
        grad_gate_low = grad_gate_act.astype(jnp.bfloat16)
        grad_up_low = grad_up_act.astype(jnp.bfloat16)
        grad_gate = product_tn(second, grad_gate_low)
        grad_up = product_tn(second, grad_up_low)
        grad_second = lax.psum_scatter(
            (product_nt(grad_gate_low, gate_full) + product_nt(grad_up_low, up_full)).astype(
                jnp.bfloat16
            ),
            "mp",
            scatter_dimension=0,
            tiled=True,
        ).astype(jnp.float32)
        norm_value, norm_pull = jax.vjp(rms_rows, hidden_state, ffn_gain)
        grad_state_norm, grad_ffn_gain = norm_pull(grad_second)
        grad_state = cotangent[micro_index].astype(jnp.float32) + grad_state_norm
        state_full = lax.all_gather(grad_state.astype(jnp.bfloat16), "mp", axis=0, tiled=True)
        grad_outw = product_tn(mixed, state_full)
        grad_mixed = (
            product_nt(state_full, out_full)
            .astype(jnp.bfloat16)
            .reshape(group, local_kv, repeat, head_size)
        )
        grad_queries, grad_keys, grad_values = attend_back(
            queries, keys, values, allowed, scale, kept, grad_mixed
        )
        query_value, query_pull = jax.vjp(
            lambda raw, gain: head_prepare(raw, gain, cosine, sine), query_raw, query_gain
        )
        grad_query_raw, grad_qgain = query_pull(grad_queries.reshape(group, local_heads, head_size))
        key_value, key_pull = jax.vjp(
            lambda raw, gain: head_prepare(raw, gain, cosine, sine), key_raw, key_gain
        )
        grad_key_raw, grad_kgain = key_pull(grad_keys)
        query_low = grad_query_raw.reshape(group, local_heads * head_size).astype(jnp.bfloat16)
        key_low = grad_key_raw.reshape(group, local_kv * head_size).astype(jnp.bfloat16)
        value_low = grad_values.reshape(group, local_kv * head_size).astype(jnp.bfloat16)
        grad_queryw = product_tn(normed, query_low)
        grad_keyw = product_tn(normed, key_low)
        grad_valuew = product_tn(normed, value_low)
        grad_normed = lax.psum_scatter(
            (
                product_nt(query_low, query_full)
                + product_nt(key_low, key_full)
                + product_nt(value_low, value_full)
            ).astype(jnp.bfloat16),
            "mp",
            scatter_dimension=0,
            tiled=True,
        ).astype(jnp.float32)
        first_value, first_pull = jax.vjp(rms_rows, resid, norm_gain)
        grad_resid_norm, grad_norm_gain = first_pull(grad_normed)
        input_grads.append((grad_state + grad_resid_norm).astype(jnp.bfloat16))
        local_grads = (
            grad_queryw,
            grad_keyw,
            grad_valuew,
            grad_gate,
            grad_up,
            grad_outw,
            grad_down,
        )
        totals = tuple((a + b for a, b in zip(totals, local_grads)))
        gain_totals = (
            gain_totals[0] + grad_norm_gain,
            gain_totals[1] + grad_ffn_gain,
            gain_totals[2] + grad_qgain,
            gain_totals[3] + grad_kgain,
        )
    finals = reduce_grads(totals)
    gains = lax.psum((gain_totals[0], gain_totals[1], gain_totals[2], gain_totals[3]), ("dp", "mp"))
    return (
        jnp.stack(outputs),
        jnp.stack(input_grads),
        finals[0],
        finals[1],
        finals[2],
        finals[5],
        finals[3],
        finals[4],
        finals[6],
        gains[0],
        gains[1],
        gains[2],
        gains[3],
    )


def solution(mesh):
    return jax.shard_map(
        local,
        mesh=mesh,
        in_specs=(
            P(None, ("dp", "mp"), None),
            P(None, "dp"),
            P(None, ("dp", "mp"), None),
            P("dp", "mp"),
            P("dp", "mp"),
            P("dp", "mp"),
            P("mp", "dp"),
            P("dp", "mp"),
            P("dp", "mp"),
            P("mp", "dp"),
            P(),
            P(),
            P(),
            P(),
        ),
        out_specs=(
            P(None, ("dp", "mp"), None),
            P(None, ("dp", "mp"), None),
            P("dp", "mp"),
            P("dp", "mp"),
            P("dp", "mp"),
            P("mp", "dp"),
            P("dp", "mp"),
            P("dp", "mp"),
            P("mp", "dp"),
            P(),
            P(),
            P(),
            P(),
        ),
        check_vma=False,
    )
```

profile of v0, /device:TPU:1, one launch (start us, length us, event | category | flops | bytes accessed | tf_op | source)
XLA Modules:
  0.0 1344.0 jit_solution(1859966111004242874)
XLA Ops:
  15.9 27.8 %all_gather.55 = bf16[1024,128]{1,0:T(8,128)(2,1)S(1)} all-gather(bf16[64,128]{1,0:T(8,128)(2,1)} %param.17), channel_id=1, replica_groups=mesh['dp'=16,'mp'=8] {'dp'}, dimensions={0}, use_global_device_ids=true | all-gather | bytes 278528 | tf_op jit(solution)/shard_map/all_gather | solution.py:54
  64.7 24.2 %all_gather.53 = bf16[1024,64]{1,0:T(8,128)(2,1)S(1)} all-gather(bf16[64,64]{1,0:T(8,128)(2,1)} %param.19), channel_id=1, replica_groups=mesh['dp'=16,'mp'=8] {'dp'}, dimensions={0}, use_global_device_ids=true | all-gather | bytes 139264 | tf_op jit(solution)/shard_map/all_gather | solution.py:56
  132.2 29.4 %reduce-scatter.20.cloned.1.call-done = bf16[64,1024]{1,0:T(8,128)(2,1)} async-done(((bf16[512,1024]{1,0:T(8,128)(2,1)}), bf16[64,1024]{1,0:T(8,128)(2,1)}) %reduce-scatter.20.cloned.1.call-update) | async-done | bytes 131088 | tf_op jit(solution)/shard_map/reduce_scatter | solution.py:194
  161.6 41.9 %reduce-scatter.16.cloned.1.call-done = bf16[64,1024]{1,0:T(8,128)(2,1)} async-done(((bf16[512,1024]{1,0:T(8,128)(2,1)}), bf16[64,1024]{1,0:T(8,128)(2,1)}) %reduce-scatter.16.cloned.1.call-update) | async-done | bytes 131088 | tf_op jit(solution)/shard_map/reduce_scatter | solution.py:194
  211.8 35.1 %all-gather.16.cloned.1.call-done = bf16[512,1024]{1,0:T(8,128)(2,1)} async-done(((bf16[64,1024]{1,0:T(8,128)(2,1)}), bf16[512,1024]{1,0:T(8,128)(2,1)}) %all-gather.16.cloned.1.call-update) | async-done | bytes 1048592 | tf_op jit(solution)/shard_map/all_gather | solution.py:198
  250.4 48.9 %all-gather.18.cloned.1.call-done = bf16[1024,576]{1,0:T(8,128)(2,1)} async-done(((bf16[64,576]{1,0:T(8,128)(2,1)}), bf16[1024,576]{1,0:T(8,128)(2,1)}) %all-gather.18.cloned.1.call-update) | async-done | bytes 1179664 | tf_op jit(solution)/shard_map/all_gather | solution.py:57
  302.8 33.3 %all-gather.32.cloned.1.call-done = bf16[1,512,1024]{2,1,0:T(8,128)(2,1)} async-done(((bf16[1,64,1024]{2,1,0:T(8,128)(2,1)}), bf16[1,512,1024]{2,1,0:T(8,128)(2,1)}) %all-gather.32.cloned.1.call-update) | async-done | bytes 1048592 | tf_op jit(solution)/shard_map/all_gather | solution.py:206
  336.1 52.5 %all-gather.22.cloned.1.call-done = bf16[576,1024]{0,1:T(8,128)(2,1)} async-done(((bf16[576,64]{0,1:T(8,128)(2,1)}), bf16[576,1024]{0,1:T(8,128)(2,1)}) %all-gather.22.cloned.1.call-update) | async-done | bytes 1179664 | tf_op jit(solution)/shard_map/all_gather | solution.py:62
  397.0 39.4 %all-gather.26.cloned.1.call-done = bf16[512,1024]{1,0:T(8,128)(2,1)} async-done(((bf16[64,1024]{1,0:T(8,128)(2,1)}), bf16[512,1024]{1,0:T(8,128)(2,1)}) %all-gather.26.cloned.1.call-update) | async-done | bytes 1048592 | tf_op jit(solution)/shard_map/all_gather | solution.py:198
  441.9 34.7 %all-gather.34.cloned.1.call-done = bf16[1,512,1024]{2,1,0:T(8,128)(2,1)} async-done(((bf16[1,64,1024]{2,1,0:T(8,128)(2,1)}), bf16[1,512,1024]{2,1,0:T(8,128)(2,1)}) %all-gather.34.cloned.1.call-update) | async-done | bytes 1048592 | tf_op jit(solution)/shard_map/all_gather | solution.py:206
  488.6 36.9 %reduce-scatter.28.cloned.1.call-done = bf16[64,1024]{1,0:T(8,128)(2,1)} async-done(((bf16[512,1024]{1,0:T(8,128)(2,1)}), bf16[64,1024]{1,0:T(8,128)(2,1)}) %reduce-scatter.28.cloned.1.call-update) | async-done | bytes 131088 | tf_op jit(solution)/shard_map/reduce_scatter | solution.py:217
  529.6 38.2 %reduce-scatter.22.cloned.1.call-done = bf16[64,1024]{1,0:T(8,128)(2,1)} async-done(((bf16[512,1024]{1,0:T(8,128)(2,1)}), bf16[64,1024]{1,0:T(8,128)(2,1)}) %reduce-scatter.22.cloned.1.call-update) | async-done | bytes 131088 | tf_op jit(solution)/shard_map/reduce_scatter | solution.py:202
  618.0 34.0 %all-gather.30.cloned.1.call-done = bf16[512,1024]{1,0:T(8,128)(2,1)} async-done(((bf16[64,1024]{1,0:T(8,128)(2,1)}), bf16[512,1024]{1,0:T(8,128)(2,1)}) %all-gather.30.cloned.1.call-update) | async-done | bytes 1048592 | tf_op jit(solution)/shard_map/all_gather | solution.py:228
  693.9 31.8 %reduce-scatter.44.cloned.1.call-done = bf16[576,64]{0,1:T(8,128)(2,1)} async-done(((bf16[576,1024]{0,1:T(8,128)(2,1)}), bf16[576,64]{0,1:T(8,128)(2,1)}) %reduce-scatter.44.cloned.1.call-update) | async-done | bytes 73744 | tf_op jit(solution)/shard_map/reduce_scatter | solution.py:89
  727.3 69.3 %reduce-scatter.42.cloned.1.call-done = bf16[64,576]{1,0:T(8,128)(2,1)} async-done(((bf16[1024,576]{1,0:T(8,128)(2,1)}), bf16[64,576]{1,0:T(8,128)(2,1)}) %reduce-scatter.42.cloned.1.call-update) | async-done | bytes 73744 | tf_op jit(solution)/shard_map/reduce_scatter | solution.py:81
  798.2 69.1 %reduce-scatter.40.cloned.1.call-done = bf16[64,576]{1,0:T(8,128)(2,1)} async-done(((bf16[1024,576]{1,0:T(8,128)(2,1)}), bf16[64,576]{1,0:T(8,128)(2,1)}) %reduce-scatter.40.cloned.1.call-update) | async-done | bytes 73744 | tf_op jit(solution)/shard_map/reduce_scatter | solution.py:78
  868.9 66.4 %reduce-scatter.36.cloned.1.call-done = bf16[64,64]{1,0:T(8,128)(2,1)} async-done(((bf16[1024,64]{1,0:T(8,128)(2,1)}), bf16[64,64]{1,0:T(8,128)(2,1)}) %reduce-scatter.36.cloned.1.call-update) | async-done | bytes 8208 | tf_op jit(solution)/shard_map/reduce_scatter | solution.py:75
  936.7 66.9 %reduce-scatter.34.cloned.1.call-done = bf16[64,64]{1,0:T(8,128)(2,1)} async-done(((bf16[1024,64]{1,0:T(8,128)(2,1)}), bf16[64,64]{1,0:T(8,128)(2,1)}) %reduce-scatter.34.cloned.1.call-update) | async-done | bytes 8208 | tf_op jit(solution)/shard_map/reduce_scatter | solution.py:72
  1004.9 66.9 %reduce-scatter.38.cloned.1.call-done = bf16[128,64]{0,1:T(8,128)(2,1)} async-done(((bf16[128,1024]{0,1:T(8,128)(2,1)}), bf16[128,64]{0,1:T(8,128)(2,1)}) %reduce-scatter.38.cloned.1.call-update) | async-done | bytes 16400 | tf_op jit(solution)/shard_map/reduce_scatter | solution.py:86
  1073.2 67.5 %reduce-scatter.32.cloned.1.call-done = bf16[64,128]{1,0:T(8,128)(2,1)} async-done(((bf16[1024,128]{1,0:T(8,128)(2,1)}), bf16[64,128]{1,0:T(8,128)(2,1)}) %reduce-scatter.32.cloned.1.call-update) | async-done | bytes 16400 | tf_op jit(solution)/shard_map/reduce_scatter | solution.py:69
  1142.0 38.4 %reduce-scatter.30.cloned.1.call-done = bf16[64,1024]{1,0:T(8,128)(2,1)} async-done(((bf16[512,1024]{1,0:T(8,128)(2,1)}), bf16[64,1024]{1,0:T(8,128)(2,1)}) %reduce-scatter.30.cloned.1.call-update) | async-done | bytes 131088 | tf_op jit(solution)/shard_map/reduce_scatter | solution.py:252
  1180.4 42.6 %reduce-scatter.26.cloned.1.call-done = bf16[64,1024]{1,0:T(8,128)(2,1)} async-done(((bf16[512,1024]{1,0:T(8,128)(2,1)}), bf16[64,1024]{1,0:T(8,128)(2,1)}) %reduce-scatter.26.cloned.1.call-update) | async-done | bytes 131088 | tf_op jit(solution)/shard_map/reduce_scatter | solution.py:252
  1225.5 39.8 %reduce-scatter.18.cloned.1.call-done = bf16[64,1024]{1,0:T(8,128)(2,1)} async-done(((bf16[512,1024]{1,0:T(8,128)(2,1)}), bf16[64,1024]{1,0:T(8,128)(2,1)}) %reduce-scatter.18.cloned.1.call-update) | async-done | bytes 131088 | tf_op jit(solution)/shard_map/reduce_scatter | solution.py:202
  1268.0 68.2 %all-reduce.8 = (f32[1024]{0:T(1024)}, f32[1024]{0:T(1024)}, f32[64]{0:T(128)}, f32[64]{0:T(128)}) all-reduce(f32[1024]{0:T(1024)S(1)} %add.294, f32[1024]{0:T(1024)S(1)} %add.295, f32[64]{0:T(128)S(1)} %add.296, f32[64]{0:T(128)S(1)} %add.297), channel_id=1, replica_groups=mesh['dp'=16,'mp'=8] {'dp','mp'}, use_global_device_ids=true, to_apply=%region_43.44 | all-reduce | flops 2176 | bytes 17408 | tf_op jit(solution)/shard_map/psum | solution.py:282
  (462 shorter events, 222.8 us)
Async XLA Ops:
  8.0 105.9 %all-gather.24.cloned.1.call-start = ((), (), s32[]{:S(2)}) async-start(), calls=%async_computation.22 | async-start | bytes 1179648 | tf_op jit(solution)/shard_map/all_gather | solution.py:180
  11.6 104.3 %all-gather.14.cloned.1.call-start = ((), (), s32[]{:S(2)}) async-start(), calls=%async_computation.15 | async-start | bytes 1179648 | tf_op jit(solution)/shard_map/all_gather | solution.py:180
  12.3 149.3 %reduce-scatter.20.cloned.1.call-start = ((), (), s32[]{:S(2)}) async-start(), calls=%async_computation.23 | async-start | bytes 1179648 | tf_op jit(solution)/shard_map/reduce_scatter | solution.py:194
  132.1 114.8 %all-gather.16.cloned.1.call-start = ((), (), s32[]{:S(2)}) async-start(), calls=%async_computation.17 | async-start | bytes 1179648 | tf_op jit(solution)/shard_map/all_gather | solution.py:198
  207.0 92.2 %all-gather.18.cloned.1.call-start = ((), (), s32[]{:S(2)}) async-start(), calls=%async_computation.18 | async-start | bytes 1392640 | tf_op jit(solution)/shard_map/all_gather | solution.py:57
  207.6 128.5 %all-gather.32.cloned.1.call-start = ((), (), s32[]{:S(2)}) async-start(), calls=%async_computation.39 | async-start | bytes 1179648 | tf_op jit(solution)/shard_map/all_gather | solution.py:206
  209.4 179.2 %all-gather.22.cloned.1.call-start = ((), (), s32[]{:S(2)}) async-start(), calls=%async_computation.20 | async-start | bytes 1392640 | tf_op jit(solution)/shard_map/all_gather | solution.py:62
  210.1 226.2 %all-gather.26.cloned.1.call-start = ((), (), s32[]{:S(2)}) async-start(), calls=%async_computation.24 | async-start | bytes 1179648 | tf_op jit(solution)/shard_map/all_gather | solution.py:198
  210.9 265.7 %all-gather.34.cloned.1.call-start = ((), (), s32[]{:S(2)}) async-start(), calls=%async_computation.40 | async-start | bytes 1179648 | tf_op jit(solution)/shard_map/all_gather | solution.py:206
  211.4 277.2 %reduce-scatter.24.cloned.1.call-start = ((), (), s32[]{:S(2)}) async-start(), calls=%async_computation.26 | async-start | bytes 1179648 | tf_op jit(solution)/shard_map/reduce_scatter | solution.py:217
  396.9 128.5 %reduce-scatter.28.cloned.1.call-start = ((), (), s32[]{:S(2)}) async-start(), calls=%async_computation.29 | async-start | bytes 1179648 | tf_op jit(solution)/shard_map/reduce_scatter | solution.py:217
  484.9 83.0 %reduce-scatter.22.cloned.1.call-start = ((), (), s32[]{:S(2)}) async-start(), calls=%async_computation.25 | async-start | bytes 1179648 | tf_op jit(solution)/shard_map/reduce_scatter | solution.py:202
  488.5 121.2 %all-gather.28.cloned.1.call-start = ((), (), s32[]{:S(2)}) async-start(), calls=%async_computation.27 | async-start | bytes 1179648 | tf_op jit(solution)/shard_map/all_gather | solution.py:228
  570.0 82.0 %all-gather.30.cloned.1.call-start = ((), (), s32[]{:S(2)}) async-start(), calls=%async_computation.30 | async-start | bytes 1179648 | tf_op jit(solution)/shard_map/all_gather | solution.py:228
  570.6 155.2 %reduce-scatter.44.cloned.1.call-start = ((), (), s32[]{:S(2)}) async-start(), calls=%async_computation.38 | async-start | bytes 1392640 | tf_op jit(solution)/shard_map/reduce_scatter | solution.py:89
  587.8 208.9 %reduce-scatter.42.cloned.1.call-start = ((), (), s32[]{:S(2)}) async-start(), calls=%async_computation.37 | async-start | bytes 1392640 | tf_op jit(solution)/shard_map/reduce_scatter | solution.py:81
  592.7 274.6 %reduce-scatter.40.cloned.1.call-start = ((), (), s32[]{:S(2)}) async-start(), calls=%async_computation.36 | async-start | bytes 1392640 | tf_op jit(solution)/shard_map/reduce_scatter | solution.py:78
  597.5 337.9 %reduce-scatter.36.cloned.1.call-start = ((), (), s32[]{:S(2)}) async-start(), calls=%async_computation.34 | async-start | bytes 278528 | tf_op jit(solution)/shard_map/reduce_scatter | solution.py:75
  667.3 336.3 %reduce-scatter.34.cloned.1.call-start = ((), (), s32[]{:S(2)}) async-start(), calls=%async_computation.33 | async-start | bytes 278528 | tf_op jit(solution)/shard_map/reduce_scatter | solution.py:72
  674.8 397.0 %reduce-scatter.38.cloned.1.call-start = ((), (), s32[]{:S(2)}) async-start(), calls=%async_computation.35 | async-start | bytes 278528 | tf_op jit(solution)/shard_map/reduce_scatter | solution.py:86
  680.4 460.3 %reduce-scatter.32.cloned.1.call-start = ((), (), s32[]{:S(2)}) async-start(), calls=%async_computation.32 | async-start | bytes 278528 | tf_op jit(solution)/shard_map/reduce_scatter | solution.py:69
  685.0 495.4 %reduce-scatter.30.cloned.1.call-start = ((), (), s32[]{:S(2)}) async-start(), calls=%async_computation.31 | async-start | bytes 1179648 | tf_op jit(solution)/shard_map/reduce_scatter | solution.py:252
  687.3 535.7 %reduce-scatter.26.cloned.1.call-start = ((), (), s32[]{:S(2)}) async-start(), calls=%async_computation.28 | async-start | bytes 1179648 | tf_op jit(solution)/shard_map/reduce_scatter | solution.py:252
  690.3 575.0 %reduce-scatter.18.cloned.1.call-start = ((), (), s32[]{:S(2)}) async-start(), calls=%async_computation.21 | async-start | bytes 1179648 | tf_op jit(solution)/shard_map/reduce_scatter | solution.py:202
  (136 other events, 9696.6 us)
Sparse Core Ops, SparseCore 0:
  11.7 41.1 all-gather.23
  55.1 40.2 all-gather.13
  125.9 35.6 reduce-scatter.19
  163.8 39.5 reduce-scatter.15
  397.0 46.2 reduce-scatter.23
  485.0 40.3 reduce-scatter.27
  527.8 39.9 reduce-scatter.21
Sparse Core Ops, SparseCore 1:
  134.5 45.5 all-gather.19
  207.1 39.7 all-gather.15
  249.3 50.0 all-gather.17
  301.5 34.5 all-gather.31
  338.6 50.0 all-gather.21
  390.8 45.5 all-gather.25
  438.4 38.0 all-gather.33
  570.1 39.6 all-gather.27
  611.8 40.1 all-gather.29
  655.9 69.8 reduce-scatter.43
  730.0 66.6 reduce-scatter.41
  800.6 66.7 reduce-scatter.39
  871.3 64.0 reduce-scatter.35
  939.5 64.0 reduce-scatter.33
  1007.7 64.0 reduce-scatter.37
  1076.6 64.0 reduce-scatter.31
  1143.2 37.2 reduce-scatter.29
  1183.0 40.0 reduce-scatter.25
  1225.4 39.9 reduce-scatter.17
where the time goes:
time: 1350 us; the launch traced here: 1340 us
  waiting for transfers between devices  1000 us (74%)
  blocking collectives  164 us (12%)
  matrix products  88.7 us (7%)
  other arithmetic  48.4 us (4%)
  between operations  18 us (1%)
  starting transfers between devices  13.9 us (1%)
    reduce_scatter x2, waiting for transfers between devices, local(): lax.psum_scatter((product_nt(query_low, query_full) + product_nt(key_low,...  81 us
    reduce_scatter x2, waiting for transfers between devices, local(): lax.psum_scatter(product(inner, down_full).astype(jnp.bfloat16), 'mp', sc...  78 us
    all_gather x2, waiting for transfers between devices, local(): lax.all_gather(second_local.astype(jnp.bfloat16), 'mp', axis=0, tiled=True)  74.5 us
    reduce_scatter x2, waiting for transfers between devices, local(): lax.psum_scatter(product(mixed, out_full).astype(jnp.bfloat16), 'mp', sca...  71.3 us
    reduce_scatter x1, waiting for transfers between devices, reduce_grads(): lax.psum_scatter(grads[4].astype(jnp.bfloat16), 'dp', scatter_dimension=0...  69.3 us
    reduce_scatter x1, waiting for transfers between devices, reduce_grads(): lax.psum_scatter(grads[3].astype(jnp.bfloat16), 'dp', scatter_dimension=0...  69.1 us
    psum x1, blocking collectives, local(): lax.psum((gain_totals[0], gain_totals[1], gain_totals[2], gain_totals[3])...  68.2 us
    all_gather x2, waiting for transfers between devices, local(): upstream = lax.all_gather(cotangent[micro_index], 'mp', axis=0, tiled=True)  68 us
  transfers between devices with their start and end apart: 26, of which 22 were waited for; matrix products, arithmetic and copies ran while one was open for 9% of the time, Pallas kernels for 0%

commit v1 on v0

v1 whole, which is shorter than its diff:
```python
import jax
import jax.numpy as jnp
from jax import lax
from jax.sharding import Mesh, PartitionSpec as P

eps = 1e-05
rope_base = 1000000.0
axes = ("y", "xh", "core", "z", "xl")
plane = ("y", "xh", "xl")
CORE = [(0, 1), (1, 0)]
bf16 = jnp.bfloat16
f32 = jnp.float32


def product(left, right):
    return jnp.dot(left, right, preferred_element_type=jnp.float32)


def product_nt(left, right):
    return lax.dot_general(
        left, right, (((1,), (1,)), ((), ())), preferred_element_type=jnp.float32
    )


def product_tn(left, right):
    return lax.dot_general(
        left, right, (((0,), (0,)), ((), ())), preferred_element_type=jnp.float32
    )


def rms_scale(value):
    return lax.rsqrt(jnp.mean(value * value, axis=-1, keepdims=True) + eps)


def rms_rows(value, gain):
    return value * rms_scale(value) * gain


def rotate(value, cosine, sine):
    half = value.shape[-1] // 2
    turned = jnp.concatenate([-value[..., half:], value[..., :half]], axis=-1)
    return value * cosine + turned * sine


def head_prepare(raw, gain, cosine, sine):
    return rotate(rms_rows(raw, gain), cosine, sine)


def swap(value):
    return lax.ppermute(
        value, ("core", "xl"), [(a * 2 + b, b * 2 + a) for a in range(2) for b in range(2)]
    )


def from_z(value, k):
    return lax.ppermute(value, "z", [(z, (z - k) % 4) for z in range(4)])


def swap_from_z(value, k):
    perm = [
        (a * 8 + z * 2 + b, b * 8 + ((z - k) % 4) * 2 + a)
        for a in range(2)
        for z in range(4)
        for b in range(2)
    ]
    return lax.ppermute(value, ("core", "z", "xl"), perm)


def other_core(value):
    return lax.ppermute(value, "core", CORE)


def gather_swapped(value):
    chain = jnp.concatenate([swap_from_z(value, k) for k in range(4)], axis=1)
    return jnp.concatenate([chain, other_core(chain)], axis=1)


def gather(value):
    chain = jnp.concatenate([value] + [from_z(value, k) for k in (1, 2, 3)], axis=1)
    return jnp.concatenate([chain, other_core(chain)], axis=1)


def scatter_sum(partial):
    half = partial.shape[1] // 2
    block = half // 4
    chain = partial[:, :half] + other_core(partial[:, half:].astype(bf16)).astype(f32)
    total = chain[:, :block]
    low = chain.astype(bf16)
    for k in (1, 2, 3):
        total = total + from_z(low[:, k * block : (k + 1) * block], -k).astype(f32)
    return total


def ordered(value, z, core, axis):
    shape = value.shape
    block = shape[axis] // 8
    v = value.reshape(shape[:axis] + (4, 2, block) + shape[axis + 1 :])
    v = lax.dynamic_slice_in_dim(jnp.concatenate([v, v], axis), z, 4, axis)
    v = lax.dynamic_slice_in_dim(jnp.concatenate([v, v], axis + 1), core, 2, axis + 1)
    return jnp.swapaxes(v, axis, axis + 1).reshape(shape)


def gather_heads(mixed):
    micro, group, cols = mixed.shape
    block = group // 8
    pieces = [mixed] + [from_z(mixed, k) for k in (1, 2, 3)]
    other = [other_core(p) for p in pieces]

    def roll(piece, k, flip):
        p = piece.reshape(micro, 2, 4, block, cols)
        if flip:
            p = p[:, ::-1]
        if k:
            p = jnp.concatenate([p[:, :, 4 - k :], p[:, :, : 4 - k]], axis=2)
        return p.reshape(micro, group, cols)

    return jnp.concatenate(
        [roll(p, k, False) for k, p in enumerate(pieces)]
        + [roll(p, k, True) for k, p in enumerate(other)],
        axis=2,
    )


def all_sum(value):
    value = value + other_core(value)
    for axis in ("z", ("xh", "xl"), "y"):
        value = value + sum(
            lax.ppermute(value, axis, [(i, (i + k) % 4) for i in range(4)]) for k in (1, 2, 3)
        )
    return value


def local(
    tokens,
    segment_ids,
    cotangent,
    w_query,
    w_key,
    w_value,
    w_out,
    w_gate,
    w_up,
    w_down,
    norm_gain,
    ffn_gain,
    query_gain,
    key_gain,
):
    micro, own, width = tokens.shape
    head_size = query_gain.shape[0]
    nq = w_query.shape[1]
    nk = w_key.shape[1]
    heads = nq // head_size
    group = segment_ids.shape[1]
    hidden = w_gate.shape[1]
    scale = head_size ** (-0.5)
    z = lax.axis_index("z")
    core = lax.axis_index("core")

    x_low = gather_swapped(tokens)
    segment = swap(segment_ids)
    w_att = lax.all_gather(
        swap(jnp.concatenate([w_query, w_key, w_value, w_out.T], axis=1)), plane, axis=0, tiled=True
    )
    w_qkv = w_att[:, : nq + 2 * nk]
    w_own = w_att[:, nq + 2 * nk :]
    w_out_t = jnp.concatenate([w_own] + [from_z(w_own, k) for k in (1, 2, 3)], axis=1)
    w_out_t = jnp.concatenate([w_out_t, other_core(w_out_t)], axis=1)
    upstream = gather_swapped(cotangent).reshape(micro * group, width)
    w_ffn = lax.all_gather(
        swap(jnp.concatenate([w_gate, w_up, w_down.T], axis=1)), plane, axis=0, tiled=True
    )
    w_gu = w_ffn[:, : 2 * hidden]
    w_down_t = w_ffn[:, 2 * hidden :]

    index = jnp.arange(group, dtype=jnp.int32)
    change = jnp.concatenate(
        [jnp.ones((micro, 1), dtype=bool), segment[:, 1:] != segment[:, :-1]], axis=1
    )
    start = lax.cummax(jnp.where(change, index, 0), axis=1)
    start = ordered(start, z, core, 1)
    index = ordered(index[None], z, core, 1)
    place = (index - start).astype(f32)
    freq = rope_base ** (-(jnp.arange(head_size // 2, dtype=f32) * 2.0 / head_size))
    angle = place[:, :, None] * freq
    angle = jnp.concatenate([angle, angle], axis=-1)
    cosine, sine = jnp.cos(angle)[:, :, None], jnp.sin(angle)[:, :, None]
    allowed = (start[:, :, None] == start[:, None, :]) & (index[:, :, None] >= index[:, None, :])

    x = x_low.astype(f32).reshape(micro * group, width)
    x_scale = rms_scale(x)
    normed = (x * x_scale * norm_gain).astype(bf16)
    qkv = product(normed, w_qkv).reshape(micro, group, heads + 2, head_size)
    query_raw, key_raw = qkv[:, :, :heads], qkv[:, :, heads : heads + 1]
    values = qkv[:, :, heads + 1].astype(bf16)
    prepare_q = lambda raw, gain: head_prepare(raw, gain, cosine, sine)
    queries, query_pull = jax.vjp(prepare_q, query_raw, query_gain)
    keys, key_pull = jax.vjp(prepare_q, key_raw, key_gain)
    queries = queries.astype(bf16)
    keys = keys[:, :, 0].astype(bf16)
    scores = jnp.einsum("mbrd,mkd->mrbk", queries, keys, preferred_element_type=f32) * scale
    scores = jnp.where(allowed[:, None], scores, -1e30)
    top = jnp.max(scores, axis=-1, keepdims=True)
    expo = jnp.exp(scores - top)
    total = jnp.sum(expo, axis=-1, keepdims=True)
    soft = expo / total
    soft_low = soft.astype(bf16)
    mixed = jnp.einsum("mrbk,mkd->mbrd", soft_low, values, preferred_element_type=f32)
    mixed = mixed.astype(bf16).reshape(micro, group, nq)
    mixed_full = gather_heads(mixed).reshape(micro * group, 8 * nq)
    mixed = mixed.reshape(micro * group, nq)
    state = x + product_nt(mixed_full, w_out_t)
    second = rms_rows(state, ffn_gain).astype(bf16)

    gate_up = product(second, w_gu)
    gate, up = gate_up[:, :hidden], gate_up[:, hidden:]
    sig = 1.0 / (1.0 + jnp.exp(-gate))
    silu = gate * sig
    inner = (silu * up).astype(bf16)
    grad_inner = product(upstream, w_down_t)
    grad_gate_low = (grad_inner * up * sig * (1.0 + gate * (1.0 - sig))).astype(bf16)
    grad_up_low = (grad_inner * silu).astype(bf16)
    grad_gu_low = jnp.concatenate([grad_gate_low, grad_up_low], axis=1)
    grad_second = product_nt(grad_gu_low, w_gu)
    grad_second = scatter_sum(grad_second.reshape(micro, group, width))
    state_own = state.reshape(micro, group, width)[:, :own]
    down = product_nt(inner, w_down_t)
    output = state_own + scatter_sum(down.reshape(micro, group, width))
    output = swap(output.astype(bf16))
    grad_ffn = jnp.concatenate(
        [product_tn(second, grad_gu_low), product_tn(upstream, inner)], axis=1
    ).astype(bf16)
    grad_ffn = lax.psum_scatter(grad_ffn, plane, scatter_dimension=0, tiled=True)
    grad_ffn = swap(grad_ffn).astype(f32)

    _, norm_pull = jax.vjp(rms_rows, state_own, ffn_gain)
    grad_state_norm, grad_ffn_gain = norm_pull(grad_second)
    cotangent_own = upstream.reshape(micro, group, width)[:, :own].astype(f32)
    grad_state = cotangent_own + grad_state_norm
    state_full = gather(grad_state.astype(bf16)).reshape(micro * group, width)

    grad_out = product_tn(state_full, mixed)
    grad_mixed = product(state_full, w_own).astype(bf16).reshape(micro, group, heads, head_size)
    grad_weights = jnp.einsum("mbrd,mkd->mrbk", grad_mixed, values, preferred_element_type=f32)
    center = jnp.sum(soft * grad_weights, axis=-1, keepdims=True)
    grad_scores = (soft * (grad_weights - center)).astype(bf16)
    grad_queries = (
        jnp.einsum("mrbk,mkd->mbrd", grad_scores, keys, preferred_element_type=f32) * scale
    )
    grad_keys = (
        jnp.einsum("mrbk,mbrd->mkd", grad_scores, queries, preferred_element_type=f32) * scale
    )
    grad_values = jnp.einsum("mrbk,mbrd->mkd", soft_low, grad_mixed, preferred_element_type=f32)
    grad_query_raw, grad_qgain = query_pull(grad_queries)
    grad_key_raw, grad_kgain = key_pull(grad_keys[:, :, None])
    qkv_low = jnp.concatenate(
        [
            grad_query_raw.reshape(micro * group, nq).astype(bf16),
            grad_key_raw.reshape(micro * group, nk).astype(bf16),
            grad_values.reshape(micro * group, nk).astype(bf16),
        ],
        axis=1,
    )
    grad_normed = product_nt(qkv_low, w_qkv)
    grad_norm_gain = jnp.sum(grad_normed * x * x_scale, axis=0)
    gains = all_sum(jnp.concatenate([grad_norm_gain, grad_ffn_gain, grad_qgain, grad_kgain]))
    grad_normed = scatter_sum(grad_normed.reshape(micro, group, width))
    grad_att = jnp.concatenate([product_tn(normed, qkv_low), grad_out], axis=1).astype(bf16)
    grad_att = lax.all_to_all(grad_att, plane, 0, 0, tiled=True)
    grad_att = jnp.sum(grad_att.reshape(16, width // 16, -1).astype(f32), axis=0)
    grad_att = swap(grad_att)
    x_own = x.reshape(micro, group, width)[:, :own]
    _, first_pull = jax.vjp(rms_rows, x_own, norm_gain)
    grad_resid_norm, _ = first_pull(grad_normed)
    input_grad = swap((grad_state + grad_resid_norm).astype(bf16))
    split = nq + nk
    return (
        output,
        input_grad,
        grad_att[:, :nq],
        grad_att[:, nq:split],
        grad_att[:, split : split + nk],
        grad_att[:, split + nk :].T,
        grad_ffn[:, :hidden],
        grad_ffn[:, hidden : 2 * hidden],
        grad_ffn[:, 2 * hidden :].T,
        gains[:width],
        gains[width : 2 * width],
        gains[2 * width : 2 * width + head_size],
        gains[2 * width + head_size :],
    )


def solution(mesh):
    inner = Mesh(mesh.devices.reshape(4, 2, 2, 4, 2), axes)
    dp, mp = ("y", "xh", "core"), ("z", "xl")
    rows = P(None, dp + mp, None)
    weight_in = [P(dp, mp)] * 3 + [P(mp, dp)] + [P(dp, mp)] * 2 + [P(mp, dp)]
    return jax.shard_map(
        local,
        mesh=inner,
        in_specs=tuple([rows, P(None, dp), rows] + weight_in + [P()] * 4),
        out_specs=tuple([rows, rows] + weight_in + [P()] * 4),
        check_vma=False,
    )
```

time: 1350 us -> 397 us (0.29)
  waiting for transfers between devices: 1000 us -> 44.8 us
  blocking collectives: 164 us -> 19.3 us
  local copies, waits for them, and re-layouts: 11.4 us -> 101 us
  starting transfers between devices: 13.9 us -> 99.8 us
  matrix products: 88.7 us -> 54.9 us
    reduce_scatter x15 -> x1, waiting for transfers between devices: 705 us -> 0.01 us  [local(): lax.psum_scatter(grad_ffn, plane, scatter_dimension=0, tiled=True)]
    all_gather x11 -> x1, waiting for transfers between devices: 290 us -> 0.01 us  [local(): lax.all_gather(swap(jnp.concatenate([w_gate, w_up, w_down.T], axis=1)), p...]
    ppermute x0 -> x54, starting transfers between devices: none -> 95.4 us  [the longest x7 25.6 us: swap(): lax.ppermute(value, ('core', 'xl'), [(a * 2 + b, b * 2 + a) for a in rang...]
    all_gather x4 -> x1, blocking collectives: 95.7 us -> 19.3 us  [local(): lax.all_gather(swap(jnp.concatenate([w_query, w_key, w_value, w_out.T], a...]
    psum x1 -> x0, blocking collectives: 68.2 us -> none  [local(): lax.psum((gain_totals[0], gain_totals[1], gain_totals[2], gain_totals[3])...]
    ppermute x0 -> x54, waiting for transfers between devices: none -> 42.9 us  [the longest x18 29 us: from_z(): return lax.ppermute(value, 'z', [(z, (z - k) % 4) for z in range(4)])]
    slice x3 -> x28, local copies, waits for them, and re-layouts: 2.34 us -> 30.5 us  [the longest x16 19.5 us: roll(): p = jnp.concatenate([p[:, :, 4 - k:], p[:, :, :4 - k]], axis=2)]
    concatenate x0 -> x14, local copies, waits for them, and re-layouts: none -> 20.4 us  [the longest x8 14.2 us: gather_heads(): jnp.concatenate([roll(p, k, False) for k, p in enumerate(pieces)] + [roll...]
  transfers between devices with their start and end apart: 26 -> 57, of which waited for: 22 -> 16; matrix products, arithmetic and copies ran while one was open for 9% -> 49% of each run, Pallas kernels for 0% -> 0%
where the time goes in v1:
time: 397 us; the launch traced here: 389 us
  local copies, waits for them, and re-layouts  101 us (25%)
  starting transfers between devices  99.8 us (25%)
  matrix products  54.9 us (14%)
  other arithmetic  54.3 us (14%)
  waiting for transfers between devices  44.8 us (11%)
  blocking collectives  19.3 us (5%)
  between operations  15.4 us (4%)
    ppermute x18, waiting for transfers between devices, from_z(): return lax.ppermute(value, 'z', [(z, (z - k) % 4) for z in range(4)])  29 us
    ppermute x7, starting transfers between devices, swap(): lax.ppermute(value, ('core', 'xl'), [(a * 2 + b, b * 2 + a) for a in rang...  25.6 us
    unnamed x149, local copies, waits for them, and re-layouts  25.3 us
    ppermute x8, starting transfers between devices, swap_from_z(): return lax.ppermute(value, ('core', 'z', 'xl'), perm)  22.4 us
    slice x16, local copies, waits for them, and re-layouts, roll(): p = jnp.concatenate([p[:, :, 4 - k:], p[:, :, :4 - k]], axis=2)  19.5 us
    all_gather x1, blocking collectives, local(): lax.all_gather(swap(jnp.concatenate([w_query, w_key, w_value, w_out.T], a...  19.3 us
    ppermute x18, starting transfers between devices, from_z(): return lax.ppermute(value, 'z', [(z, (z - k) % 4) for z in range(4)])  18.6 us
    ppermute x12, starting transfers between devices, other_core(): return lax.ppermute(value, 'core', CORE)  16.9 us
  transfers between devices with their start and end apart: 57, of which 16 were waited for; matrix products, arithmetic and copies ran while one was open for 49% of the time, Pallas kernels for 0%

profile of v1, /device:TPU:1, one launch (start us, length us, event | category | flops | bytes accessed | tf_op | source)
XLA Modules:
  0.0 389.1 jit_solution(14662231638465156815)
XLA Ops:
  7.2 4.5 %collective-permute-start = (bf16[2,64,1024]{2,1,0:T(8,128)(2,1)}, bf16[2,64,1024]{2,1,0:T(8,128)(2,1)S(1)}, u32[]{:S(2)}, u32[]{:S(2)}) collective-permute-start(bf16[2,64,1024]{2,1,0:T(8,128)(2,1)} %param.14), channel_id=1, source_target_pairs={{0,0},{1,8},{2,2},{3,10},{4,4},{5,12},{6,6},{7,14},{8,1},{9,9},{10... | collective-permute-start | bytes 786440 | tf_op jit(solution)/shard_map/ppermute | solution.py:66
  11.7 3.6 collective-permute-start.1
  23.2 4.6 %collective-permute-done.6 = s32[2,512]{1,0:T(2,128)S(1)} collective-permute-done((s32[2,512]{1,0:T(2,128)}, s32[2,512]{1,0:T(2,128)S(1)}, u32[]{:S(2)}, u32[]{:S(2)}) %collective-permute-start.6) | collective-permute-done | bytes 4128 | tf_op jit(solution)/shard_map/ppermute | solution.py:50
  34.8 3.6 collective-permute-start.18
  38.5 19.3 %all_gather.6 = bf16[1024,384]{1,0:T(8,128)(2,1)S(1)} all-gather(bf16[64,384]{1,0:T(8,128)(2,1)S(1)} %collective-permute-done.5), channel_id=1, replica_groups=mesh['y'=4,'xh'=2,'core'=2,'z'=4,'xl'=2] {'y','xh','xl'}, dimensions={0}, use_global_device_ids=true | all-gather | bytes 835584 | tf_op jit(solution)/shard_map/all_gather | solution.py:162
  58.9 7.4 %collective-permute-start.24 = (bf16[2,64,1024]{2,1,0:T(8,128)(2,1)}, bf16[2,64,1024]{2,1,0:T(8,128)(2,1)S(1)}, u32[]{:S(2)}, u32[]{:S(2)}) collective-permute-start(bf16[2,64,1024]{2,1,0:T(8,128)(2,1)} %param.16), channel_id=1, source_target_pairs={{0,0},{1,8},{2,2},{3,10},{4,4},{5,12},{6,6},{7,14},{8,1},{9,9},{10... | collective-permute-start | bytes 786440 | tf_op jit(solution)/shard_map/ppermute | solution.py:66
  83.4 9.7 %collective-permute-start.28 = (bf16[2,256,1024]{2,1,0:T(8,128)(2,1)}, bf16[2,256,1024]{2,1,0:T(8,128)(2,1)}, u32[]{:S(2)}, u32[]{:S(2)}) collective-permute-start(bf16[2,256,1024]{2,1,0:T(8,128)(2,1)} %pad_maximum_fusion.6), channel_id=1, source_target_pairs={{0,8},{8,0},{1,9},{9,1},{2,10},{10,2},{3,11},{11,3},{4,12},{12,4},... | collective-permute-start | bytes 3145736 | tf_op jit(solution)/shard_map/ppermute | solution.py:70
  105.6 5.5 %fusion.112 = (f32[2,2,512]{2,1,0:T(2,128)}, f32[2,2,512,512]{2,3,1,0:T(8,128)}) fusion(pred[2,512,512]{1,2,0:T(8,128)(4,1)} %compare_and_fusion, bf16[2,512,2,64]{1,3,2,0:T(8,128)(2,1)} %fusion.47, bf16[2,512,1,64]{1,3,2,0:T(8,128)(2,1)} %fusion.58), kind=kOutput, calls=%fused_computation.246 | convolution fusion | flops 138412544 | bytes 5120000 | tf_op jit(solution)/shard_map/sub | solution.py:204
  125.3 5.8 %collective-permute-done.9 = bf16[2,512,128]{2,1,0:T(8,128)(2,1)S(1)} collective-permute-done((bf16[2,512,128]{2,1,0:T(8,128)(2,1)}, bf16[2,512,128]{2,1,0:T(8,128)(2,1)S(1)}, u32[]{:S(2)}, u32[]{:S(2)}) %collective-permute-start.9) | collective-permute-done | bytes 262176 | tf_op jit(solution)/shard_map/ppermute | solution.py:56
  186.8 6.7 %multiply_reduce_fusion = (f32[1024]{0:T(1024)S(1)}, f32[1024,1024]{1,0:T(8,128)}) fusion(bf16[1024,1024]{0,1:T(8,128)(2,1)} %constant_dynamic-update-slice_fusion.5, bf16[1024,1024]{1,0:T(8,128)(2,1)} %copy-done.44, bf16[2,512,1024]{2,1,0:T(8,128)(2,1)S(1)} %constant_dynamic-update-slice_fusion), kind=kOutput, calls=%fused_computation.20 | convolution fusion | flops 2151676928 | bytes 10489856 | tf_op jit(solution)/shard_map/dot_general | solution.py:20
  194.2 5.7 %fusion.23 = f32[1024,1152]{1,0:T(8,128)S(1)} fusion(bf16[1024,1728]{1,0:T(8,128)(2,1)} %all-gather.2.cloned.1.call-done, f32[1024,1024]{1,0:T(8,128)} %get-tuple-element.86, f32[1024]{0:T(1024)} %param.25, f32[1024]{0:T(1024)} %add_rsqrt_fusion), kind=kOutput, calls=%fused_computation.48 | convolution fusion | flops 2419064832 | bytes 11280384 | tf_op jit(solution)/shard_map/dot_general | solution.py:16
  209.2 5.2 %convolution_convert_fusion = bf16[1024,1152]{1,0:T(8,128)(2,1)} fusion(bf16[1024,576]{1,0:T(8,128)(2,1)S(1)} %get-tuple-element.33, bf16[1024,576]{1,0:T(8,128)(2,1)S(1)} %get-tuple-element.32, f32[1024,1024]{1,0:T(8,128)S(1)} %copy-done.21, f32[1024]{0:T(1024)S(1)} %copy-done.41, f32[1024]{0:T(1024)S(1)} %copy-done.58), kind=kOutput, calls=%fused_computation.22 | convolution fusion | flops 2424963072 | bytes 8921088 | tf_op jit(solution)/shard_map/dot_general | solution.py:26
  224.2 5.3 %collective-permute-done.31 = bf16[2,64,1024]{2,1,0:T(8,128)(2,1)S(1)} collective-permute-done((bf16[2,64,1024]{2,1,0:T(8,128)(2,1)S(1)}, bf16[2,64,1024]{2,1,0:T(8,128)(2,1)S(1)}, u32[]{:S(2)}, u32[]{:S(2)}) %collective-permute-start.31) | collective-permute-done | bytes 262176 | tf_op jit(solution)/shard_map/ppermute | solution.py:56
  244.2 6.2 %collective-permute-done.35 = bf16[2,64,1024]{2,1,0:T(8,128)(2,1)} collective-permute-done((bf16[2,64,1024]{2,1,0:T(8,128)(2,1)}, bf16[2,64,1024]{2,1,0:T(8,128)(2,1)}, u32[]{:S(2)}, u32[]{:S(2)}) %collective-permute-start.35) | collective-permute-done | bytes 262176 | tf_op jit(solution)/shard_map/ppermute | solution.py:56
  253.5 3.8 pad_maximum_fusion
  257.4 4.3 %fusion.99 = (bf16[2,256,1024]{2,1,0:T(8,128)(2,1)}, f32[2,256,1024]{2,1,0:T(8,128)}) fusion(bf16[2,256,1024]{2,1,0:T(8,128)(2,1)} %collective-permute-done.19, f32[2,512,1024]{2,1,0:T(8,128)} %bitcast.177), kind=kLoop, calls=%fused_computation.233 | loop fusion | flops 1572864 | bytes 6291456 | tf_op jit(solution)/shard_map/convert_element_type | solution.py:88
  296.4 4.8 %fusion.10 = (f32[1024]{0:T(1024)S(1)}, bf16[1024,1024]{1,0:T(8,128)(2,1)}, f32[1024,1024]{1,0:T(8,128)}) fusion(bf16[2,512,1024]{2,1,0:T(8,128)(2,1)S(1)} %constant_dynamic-update-slice_fusion, f32[1024]{0:T(1024)S(1)} %bitcast.209, f32[1024]{0:T(1024)S(1)} %copy-done.38, bf16[1024,384]{1,0:T(8,128)(2,1)S(1)} %copy-done.2, bf16[1024,64]{1,0:T(8,128)(2,1)} %bitcast.185, ...), kind=kOutput, calls=%fused_computation.18 | convolution fusion | flops 545782784 | bytes 9449472 | tf_op jit(solution)/shard_map/dot_general | solution.py:20
  303.3 4.1 %copy.157 = bf16[1024,1024]{0,1:T(8,128)(2,1)} copy(bf16[1024,1024]{1,0:T(8,128)(2,1)} %bitcast.175) | data formatting | bytes 4194304 | tf_op jit(solution)/shard_map/reshape | solution.py:240
  307.5 3.8 collective-permute-start.46
  331.4 4.4 %all-to-all-start = ((bf16[16,64,384]{2,1,0:T(8,128)(2,1)}), bf16[16,64,384]{2,1,0:T(8,128)(2,1)}, u32[]{:S(2)}, u32[]{:S(2)}) async-start(bf16[16,64,384]{2,1,0:T(8,128)(2,1)} %pad_maximum_fusion.8), calls=%async_computation | async-start | bytes 1572864 | tf_op jit(solution)/shard_map/all_to_all | solution.py:269
  341.6 3.5 collective-permute-start.39
  354.0 7.4 %collective-permute-start.42 = (f32[64,384]{1,0:T(8,128)S(1)}, f32[64,384]{1,0:T(8,128)S(1)}, u32[]{:S(2)}, u32[]{:S(2)}) collective-permute-start(f32[64,384]{1,0:T(8,128)S(1)} %convert_reduce_fusion), channel_id=1, source_target_pairs={{0,0},{1,8},{8,1},{9,9},{2,2},{3,10},{10,3},{11,11},{4,4},{5,12},{... | collective-permute-start | bytes 294920 | tf_op jit(solution)/shard_map/ppermute | solution.py:50
  365.7 3.7 collective-permute-start.23
  372.0 3.6 collective-permute-start.43
  (392 shorter events, 237.1 us)
Async XLA Ops:
  7.2 187.0 %all-gather.2.cloned.1.call-start = ((), (), s32[]{:S(2)}) async-start(), calls=%async_computation.2 | async-start | bytes 3899392 | tf_op jit(solution)/shard_map/all_gather | solution.py:170
  7.2 59.1 %collective-permute-start = (bf16[2,64,1024]{2,1,0:T(8,128)(2,1)}, bf16[2,64,1024]{2,1,0:T(8,128)(2,1)S(1)}, u32[]{:S(2)}, u32[]{:S(2)}) collective-permute-start(bf16[2,64,1024]{2,1,0:T(8,128)(2,1)} %param.14), channel_id=1, source_target_pairs={{0,0},{1,8},{2,2},{3,10},{4,4},{5,12},{6,6},{7,14},{8,1},{9,9},{10... | collective-permute-start | bytes 786440 | tf_op jit(solution)/shard_map/ppermute | solution.py:66
  11.7 57.2 %collective-permute-start.1 = (bf16[2,64,1024]{2,1,0:T(8,128)(2,1)}, bf16[2,64,1024]{2,1,0:T(8,128)(2,1)S(1)}, u32[]{:S(2)}, u32[]{:S(2)}) collective-permute-start(bf16[2,64,1024]{2,1,0:T(8,128)(2,1)} %param.14), channel_id=1, source_target_pairs={{0,6},{1,14},{2,0},{3,8},{4,2},{5,10},{6,4},{7,12},{8,7},{9,15},{1... | collective-permute-start | bytes 786440 | tf_op jit(solution)/shard_map/ppermute | solution.py:66
  15.3 55.1 %collective-permute-start.2 = (bf16[2,64,1024]{2,1,0:T(8,128)(2,1)}, bf16[2,64,1024]{2,1,0:T(8,128)(2,1)S(1)}, u32[]{:S(2)}, u32[]{:S(2)}) collective-permute-start(bf16[2,64,1024]{2,1,0:T(8,128)(2,1)} %param.14), channel_id=1, source_target_pairs={{0,4},{1,12},{2,6},{3,14},{4,0},{5,8},{6,2},{7,10},{8,5},{9,13},{1... | collective-permute-start | bytes 786440 | tf_op jit(solution)/shard_map/ppermute | solution.py:66
  16.4 55.6 %collective-permute-start.3 = (bf16[2,64,1024]{2,1,0:T(8,128)(2,1)}, bf16[2,64,1024]{2,1,0:T(8,128)(2,1)S(1)}, u32[]{:S(2)}, u32[]{:S(2)}) collective-permute-start(bf16[2,64,1024]{2,1,0:T(8,128)(2,1)} %param.14), channel_id=1, source_target_pairs={{0,2},{1,10},{2,4},{3,12},{4,6},{5,14},{6,0},{7,8},{8,3},{9,11},{1... | collective-permute-start | bytes 786440 | tf_op jit(solution)/shard_map/ppermute | solution.py:66
  34.8 24.0 %collective-permute-start.18 = (bf16[64,1728]{1,0:T(8,128)(2,1)S(1)}, bf16[64,1728]{1,0:T(8,128)(2,1)S(1)}, u32[]{:S(2)}, u32[]{:S(2)}) collective-permute-start(bf16[64,1728]{1,0:T(8,128)(2,1)S(1)} %concatenate.178), channel_id=1, source_target_pairs={{0,0},{1,8},{8,1},{9,9},{2,2},{3,10},{10,3},{11,11},{4,4},{5,12},{... | collective-permute-start | bytes 663560 | tf_op jit(solution)/shard_map/ppermute | solution.py:50
  58.9 15.4 %collective-permute-start.24 = (bf16[2,64,1024]{2,1,0:T(8,128)(2,1)}, bf16[2,64,1024]{2,1,0:T(8,128)(2,1)S(1)}, u32[]{:S(2)}, u32[]{:S(2)}) collective-permute-start(bf16[2,64,1024]{2,1,0:T(8,128)(2,1)} %param.16), channel_id=1, source_target_pairs={{0,0},{1,8},{2,2},{3,10},{4,4},{5,12},{6,6},{7,14},{8,1},{9,9},{10... | collective-permute-start | bytes 786440 | tf_op jit(solution)/shard_map/ppermute | solution.py:66
  71.9 300.1 %reduce-scatter.2.cloned.1.call-start = ((), (), s32[]{:S(2)}) async-start(), calls=%async_computation.3 | async-start | bytes 3899392 | tf_op jit(solution)/shard_map/reduce_scatter | solution.py:233
  72.0 22.4 %collective-permute-start.14 = (bf16[1024,128]{1,0:T(8,128)(2,1)S(1)}, bf16[1024,128]{1,0:T(8,128)(2,1)S(1)}, u32[]{:S(2)}, u32[]{:S(2)}) collective-permute-start(bf16[1024,128]{1,0:T(8,128)(2,1)S(1)} %get-tuple-element.48), channel_id=1, source_target_pairs={{0,6},{2,0},{4,2},{6,4},{1,7},{3,1},{5,3},{7,5},{8,14},{10,8},{12,... | collective-permute-start | bytes 786440 | tf_op jit(solution)/shard_map/ppermute | solution.py:56
  74.2 20.1 %collective-permute-start.15 = (bf16[1024,128]{1,0:T(8,128)(2,1)S(1)}, bf16[1024,128]{1,0:T(8,128)(2,1)S(1)}, u32[]{:S(2)}, u32[]{:S(2)}) collective-permute-start(bf16[1024,128]{1,0:T(8,128)(2,1)S(1)} %get-tuple-element.48), channel_id=1, source_target_pairs={{0,4},{2,6},{4,0},{6,2},{1,5},{3,7},{5,1},{7,3},{8,12},{10,14},{12... | collective-permute-start | bytes 786440 | tf_op jit(solution)/shard_map/ppermute | solution.py:56
  75.7 19.9 %collective-permute-start.16 = (bf16[1024,128]{1,0:T(8,128)(2,1)S(1)}, bf16[1024,128]{1,0:T(8,128)(2,1)S(1)}, u32[]{:S(2)}, u32[]{:S(2)}) collective-permute-start(bf16[1024,128]{1,0:T(8,128)(2,1)S(1)} %get-tuple-element.48), channel_id=1, source_target_pairs={{0,2},{2,4},{4,6},{6,0},{1,3},{3,5},{5,7},{7,1},{8,10},{10,12},{12... | collective-permute-start | bytes 786440 | tf_op jit(solution)/shard_map/ppermute | solution.py:56
  79.9 19.6 %collective-permute-start.4 = (bf16[2,256,1024]{2,1,0:T(8,128)(2,1)S(1)}, bf16[2,256,1024]{2,1,0:T(8,128)(2,1)S(1)}, u32[]{:S(2)}, u32[]{:S(2)}) collective-permute-start(bf16[2,256,1024]{2,1,0:T(8,128)(2,1)S(1)} %pad_maximum_fusion.4), channel_id=1, source_target_pairs={{0,8},{8,0},{1,9},{9,1},{2,10},{10,2},{3,11},{11,3},{4,12},{12,4},... | collective-permute-start | bytes 3145736 | tf_op jit(solution)/shard_map/ppermute | solution.py:70
  83.4 35.7 %collective-permute-start.28 = (bf16[2,256,1024]{2,1,0:T(8,128)(2,1)}, bf16[2,256,1024]{2,1,0:T(8,128)(2,1)}, u32[]{:S(2)}, u32[]{:S(2)}) collective-permute-start(bf16[2,256,1024]{2,1,0:T(8,128)(2,1)} %pad_maximum_fusion.6), channel_id=1, source_target_pairs={{0,8},{8,0},{1,9},{9,1},{2,10},{10,2},{3,11},{11,3},{4,12},{12,4},... | collective-permute-start | bytes 3145736 | tf_op jit(solution)/shard_map/ppermute | solution.py:70
  96.9 27.1 %collective-permute-start.17 = (bf16[1024,512]{1,0:T(8,128)(2,1)}, bf16[1024,512]{1,0:T(8,128)(2,1)}, u32[]{:S(2)}, u32[]{:S(2)}) collective-permute-start(bf16[1024,512]{1,0:T(8,128)(2,1)} %pad_maximum_fusion.5), channel_id=1, source_target_pairs={{0,8},{8,0},{1,9},{9,1},{2,10},{10,2},{3,11},{11,3},{4,12},{12,4},... | collective-permute-start | bytes 3145736 | tf_op jit(solution)/shard_map/ppermute | solution.py:70
  116.4 20.4 %collective-permute-start.8 = (bf16[2,512,128]{2,1,0:T(8,128)(2,1)}, bf16[2,512,128]{2,1,0:T(8,128)(2,1)}, u32[]{:S(2)}, u32[]{:S(2)}) collective-permute-start(bf16[2,512,128]{2,1,0:T(8,128)(2,1)} %copy.129), channel_id=1, source_target_pairs={{0,4},{2,6},{4,0},{6,2},{1,5},{3,7},{5,1},{7,3},{8,12},{10,14},{12... | collective-permute-start | bytes 786440 | tf_op jit(solution)/shard_map/ppermute | solution.py:56
  119.1 30.0 %collective-permute-start.10 = (bf16[2,512,128]{2,1,0:T(8,128)(2,1)}, bf16[2,512,128]{2,1,0:T(8,128)(2,1)}, u32[]{:S(2)}, u32[]{:S(2)}) collective-permute-start(bf16[2,512,128]{2,1,0:T(8,128)(2,1)} %copy.129), channel_id=1, source_target_pairs={{0,8},{8,0},{1,9},{9,1},{2,10},{10,2},{3,11},{11,3},{4,12},{12,4},... | collective-permute-start | bytes 786440 | tf_op jit(solution)/shard_map/ppermute | solution.py:70
  146.5 20.5 %collective-permute-start.12 = (bf16[2,512,128]{2,1,0:T(8,128)(2,1)}, bf16[2,512,128]{2,1,0:T(8,128)(2,1)}, u32[]{:S(2)}, u32[]{:S(2)}) collective-permute-start(bf16[2,512,128]{2,1,0:T(8,128)(2,1)} %collective-permute-done.8), channel_id=1, source_target_pairs={{0,8},{8,0},{1,9},{9,1},{2,10},{10,2},{3,11},{11,3},{4,12},{12,4},... | collective-permute-start | bytes 786440 | tf_op jit(solution)/shard_map/ppermute | solution.py:70
  220.9 36.5 %collective-permute-start.19 = (bf16[2,256,1024]{2,1,0:T(8,128)(2,1)}, bf16[2,256,1024]{2,1,0:T(8,128)(2,1)}, u32[]{:S(2)}, u32[]{:S(2)}) collective-permute-start(bf16[2,256,1024]{2,1,0:T(8,128)(2,1)} %slice.416), channel_id=1, source_target_pairs={{0,8},{8,0},{1,9},{9,1},{2,10},{10,2},{3,11},{11,3},{4,12},{12,4},... | collective-permute-start | bytes 3145736 | tf_op jit(solution)/shard_map/ppermute | solution.py:70
  303.3 59.5 %collective-permute-start.20 = (bf16[2,64,1024]{2,1,0:T(8,128)(2,1)}, bf16[2,64,1024]{2,1,0:T(8,128)(2,1)}, u32[]{:S(2)}, u32[]{:S(2)}) collective-permute-start(bf16[2,64,1024]{2,1,0:T(8,128)(2,1)} %get-tuple-element.45), channel_id=1, source_target_pairs={{0,2},{2,4},{4,6},{6,0},{1,3},{3,5},{5,7},{7,1},{8,10},{10,12},{12... | collective-permute-start | bytes 786440 | tf_op jit(solution)/shard_map/ppermute | solution.py:56
  319.1 19.0 %collective-permute-start.37 = (bf16[2,256,1024]{2,1,0:T(8,128)(2,1)}, bf16[2,256,1024]{2,1,0:T(8,128)(2,1)}, u32[]{:S(2)}, u32[]{:S(2)}) collective-permute-start(bf16[2,256,1024]{2,1,0:T(8,128)(2,1)} %slice.414), channel_id=1, source_target_pairs={{0,8},{8,0},{1,9},{9,1},{2,10},{10,2},{3,11},{11,3},{4,12},{12,4},... | collective-permute-start | bytes 3145736 | tf_op jit(solution)/shard_map/ppermute | solution.py:70
  331.4 16.2 %all-to-all-start = ((bf16[16,64,384]{2,1,0:T(8,128)(2,1)}), bf16[16,64,384]{2,1,0:T(8,128)(2,1)}, u32[]{:S(2)}, u32[]{:S(2)}) async-start(bf16[16,64,384]{2,1,0:T(8,128)(2,1)} %pad_maximum_fusion.8), calls=%async_computation | async-start | bytes 1572864 | tf_op jit(solution)/shard_map/all_to_all | solution.py:269
  335.8 27.0 %collective-permute-start.21 = (bf16[2,64,1024]{2,1,0:T(8,128)(2,1)}, bf16[2,64,1024]{2,1,0:T(8,128)(2,1)}, u32[]{:S(2)}, u32[]{:S(2)}) collective-permute-start(bf16[2,64,1024]{2,1,0:T(8,128)(2,1)} %get-tuple-element.47), channel_id=1, source_target_pairs={{0,4},{2,6},{4,0},{6,2},{1,5},{3,7},{5,1},{7,3},{8,12},{10,14},{12... | collective-permute-start | bytes 786440 | tf_op jit(solution)/shard_map/ppermute | solution.py:56
  345.2 16.2 %collective-permute-start.40 = (bf16[2,64,1024]{2,1,0:T(8,128)(2,1)}, bf16[2,64,1024]{2,1,0:T(8,128)(2,1)}, u32[]{:S(2)}, u32[]{:S(2)}) collective-permute-start(bf16[2,64,1024]{2,1,0:T(8,128)(2,1)} %get-tuple-element.40), channel_id=1, source_target_pairs={{0,6},{2,0},{4,2},{6,4},{1,7},{3,1},{5,3},{7,5},{8,14},{10,8},{12,... | collective-permute-start | bytes 786440 | tf_op jit(solution)/shard_map/ppermute | solution.py:56
  354.0 17.4 %collective-permute-start.42 = (f32[64,384]{1,0:T(8,128)S(1)}, f32[64,384]{1,0:T(8,128)S(1)}, u32[]{:S(2)}, u32[]{:S(2)}) collective-permute-start(f32[64,384]{1,0:T(8,128)S(1)} %convert_reduce_fusion), channel_id=1, source_target_pairs={{0,0},{1,8},{8,1},{9,9},{2,2},{3,10},{10,3},{11,11},{4,4},{5,12},{... | collective-permute-start | bytes 294920 | tf_op jit(solution)/shard_map/ppermute | solution.py:50
  (95 other events, 696.3 us)
Sparse Core Ops, SparseCore 0:
  72.1 47.4 all-gather.1
  257.5 71.6 reduce-scatter.1
